TPU v7x, 256 devices: a whole 4x4x8 slice. The times are simulated.
256 devices in a mesh: row: 8 (over z), col: 16 (over y, x), layer: 2 (over core).
Axes of the slice: x: 4, y: 4, z: 8, core: 2. Of those that a mesh axis runs over, the one named last changes fastest.
Arguments:
- density: bfloat16 [8192, 8192], P('row', ('col', 'layer')), may hold values from -3 to 3
- block_mask: int32 [64, 64], P('row', ('col', 'layer')), may hold values from 0 to 1, as said below
- keep_mask: int32 [64, 64], P('row', ('col', 'layer')), may hold values 0 or 1
- branch_flag: int32 [64], P('row'), may hold values from 0 to 1
Outputs:
- updated: float32 [8192, 8192], P('row', ('col', 'layer'))
- trace_new: float32 [], replicated
Inputs may be any that keep to these rules, and one draw needn't show every extreme that they name: `block_mask`: symmetric, 1 on the diagonal; 1 where two blocks' centres in a periodic box lie within a cutoff distance of each other, else 0; block labels are in no spatial order. `keep_mask`: 0 or 1 for each block.
All inputs are finite; a program needn't handle non-finite values.
Results may differ from a plain program's by a relative error of at most 0.0004.
Values may be sent and summed in bfloat16 or wider, within the bound.
No kernel may reach another device: no remote copies, remote signals or barrier semaphores. Data moves between devices by JAX's collectives and lax.ppermute only.
A program may use at most 64 MiB of HBM per device.

v0:
```python
import functools
import jax
import jax.numpy as jnp
from jax import lax
from jax.sharding import Mesh
from jax.sharding import PartitionSpec as P

BLK = 128
COL = ("col_0", "col_1")
ROW_COL_LAYER = ("row", "col_0", "col_1", "layer")
COL_LAYER = ("col_0", "col_1", "layer")


def partner(value, axis, stride):
    mask = 2**stride
    pairs = [(source, source ^ mask) for source in range(lax.axis_size(axis))]
    return lax.ppermute(value, axis, pairs)


def split_up(value, dim, devices):
    shape = value.shape
    pieces = value.reshape(*shape[:dim], devices, shape[dim] // devices, *shape[dim + 1 :])
    return jnp.moveaxis(pieces, dim, 0)


def sum_at_owner(value, axis, dim):
    devices = lax.axis_size(axis)
    pieces = lax.all_to_all(split_up(value, dim, devices), axis, 0, 0, tiled=True)
    return jnp.sum(pieces, axis=0)


def over_axes(value, axes):
    return functools.reduce(lax.psum, axes, value)


def expand_mask(block_mask):
    return jnp.repeat(jnp.repeat(block_mask, BLK, axis=0), BLK, axis=1)


def on_device(density, block_mask, keep_mask, branch_flag):
    row_count = density.shape[0]
    col_width = density.shape[1]
    masked = density * expand_mask(block_mask).astype(jnp.bfloat16)
    col_panel = lax.all_gather(masked, "row", axis=0, tiled=True)
    layer_index = lax.axis_index("layer")
    col_groups = lax.axis_size(COL)
    grouped = col_panel.reshape(col_groups, 2, col_width, col_width)
    own_rows = lax.dynamic_index_in_dim(grouped, layer_index, 1, keepdims=False)
    outgoing = lax.dynamic_index_in_dim(grouped, 1 - layer_index, 1, keepdims=False)
    peer_rows = partner(outgoing, "layer", 0)
    own_rows = own_rows.reshape(col_groups * col_width, col_width)
    peer_rows = peer_rows.reshape(col_groups * col_width, col_width)
    lead_part = jnp.where(layer_index == 0, own_rows, peer_rows)
    tail_part = jnp.where(layer_index == 0, peer_rows, own_rows)
    inner_panel = jnp.concatenate([lead_part, tail_part], axis=1)
    partial_value = jnp.dot(
        lax.all_gather(masked, COL, axis=1, tiled=True),
        inner_panel,
        preferred_element_type=jnp.float32,
    )
    product = sum_at_owner(partial_value, "layer", 1)
    doubled = 2.0 * masked.astype(jnp.float32) - product
    flag_rows = jnp.repeat(branch_flag, BLK)[:, None]
    chosen = jnp.where(flag_rows == 1, product, doubled)
    updated = chosen * expand_mask(keep_mask).astype(jnp.float32)
    row_anchor = lax.axis_index("row") * row_count
    col_anchor = (
        lax.axis_index(COL) * lax.axis_size("layer") + lax.axis_index("layer")
    ) * col_width
    row_ids = row_anchor + jnp.arange(row_count, dtype=jnp.int32)[:, None]
    col_ids = col_anchor + jnp.arange(col_width, dtype=jnp.int32)[None, :]
    local_trace = jnp.sum(jnp.where(row_ids == col_ids, updated, 0.0))
    trace_new = over_axes(local_trace, ROW_COL_LAYER)
    return (updated, trace_new)


def solution(mesh):
    split = Mesh(
        mesh.devices.reshape(mesh.shape["row"], 4, 4, mesh.shape["layer"]),
        ("row", "col_0", "col_1", "layer"),
    )
    in_specs = (P("row", COL_LAYER), P("row", COL_LAYER), P("row", COL_LAYER), P("row"))
    out_specs = (P("row", COL_LAYER), P())
    return jax.shard_map(
        on_device, mesh=split, in_specs=in_specs, out_specs=out_specs, check_vma=False
    )
```

profile of v0, /device:TPU:1, one launch (start us, length us, event | category | flops | bytes accessed | tf_op | source)
XLA Modules:
  0.0 212.9 jit_solution(15898853218652076611)
XLA Ops:
  7.2 0.0 all-gather.5.cloned.1.call-start
  7.2 1.2 copy.10
  8.5 0.7 convert_element_type.25
  9.1 0.1 broadcast_bitcast_fusion.1
  9.2 0.8 bitcast_multiply_fusion
  10.1 0.0 all-gather.5.cloned.1.call-update
  10.1 0.0 all-gather.3.cloned.1.call-start
  10.1 0.7 all-gather.3.cloned.1.call-update
  10.9 58.0 %all-gather.5.cloned.1.call-done = bf16[8192,256]{0,1:T(8,128)(2,1)} async-done(((bf16[1024,256]{0,1:T(8,128)(2,1)}), bf16[8192,256]{0,1:T(8,128)(2,1)}) %all-gather.5.cloned.1.call-update) | async-done | bytes 4194320 | tf_op jit(solution)/shard_map/all_gather | solution.py:44
  68.9 7.8 %reshape.44 = bf16[16,2,256,256]{2,1,0,3:T(2,128)(2,1)} reshape(bf16[8192,256]{0,1:T(8,128)(2,1)} %all-gather.5.cloned.1.call-done) | data formatting | bytes 8388608 | tf_op jit(solution)/shard_map/reshape | solution.py:47
  76.7 13.4 %constant_dynamic-slice_fusion.1 = (bf16[16,1,256,256]{2,1,0,3:T(2,128)(2,1)}, bf16[16,1,256,256]{2,1,0,3:T(2,128)(2,1)}) fusion(bf16[16,2,256,256]{2,1,0,3:T(2,128)(2,1)} %reshape.44, s32[]{:T(128)S(6)} %select_n.28, s32[]{:T(128)S(6)} %select_n.29), kind=kLoop, calls=%fused_computation.18 | loop fusion | bytes 8388616 | tf_op jit(solution)/shard_map/jit(dynamic_index_in_dim)/dynamic_slice | solution.py:48
  90.1 10.5 %copy.15 = bf16[16,1,256,256]{3,2,0,1:T(8,128)(2,1)} copy(bf16[16,1,256,256]{2,1,0,3:T(2,128)(2,1)} %get-tuple-element.11) | data formatting | bytes 4194304
  100.6 0.7 collective-permute-start
  101.3 0.0 copy-done.1
  101.3 0.1 broadcast_bitcast_fusion
  101.4 0.0 copy-done.2
  101.4 0.1 broadcast_bitcast_fusion.2
  101.5 9.0 %copy.14 = bf16[16,1,256,256]{3,2,0,1:T(8,128)(2,1)S(1)} copy(bf16[16,1,256,256]{2,1,0,3:T(2,128)(2,1)} %get-tuple-element.10) | data formatting | bytes 4194304
  110.5 0.0 collective-permute-done
  110.5 3.8 %bitcast_select_fusion.1 = (bf16[4096,256]{1,0:T(8,128)(2,1)}, bf16[4096,256]{1,0:T(8,128)(2,1)}) fusion(bf16[16,256,256]{2,1,0:T(8,128)(2,1)} %collective-permute-done, bf16[16,1,256,256]{3,2,0,1:T(8,128)(2,1)S(1)} %copy.14, pred[]{:T(512)S(6)} %eq.35), kind=kLoop, calls=%fused_computation.5 | loop fusion | flops 2097152 | bytes 8388609 | tf_op jit(solution)/shard_map/jit(_where)/select_n | solution.py:53
  114.3 31.4 %all-gather.3.cloned.1.call-done = bf16[1024,4096]{0,1:T(8,128)(2,1)} async-done(((bf16[1024,256]{0,1:T(8,128)(2,1)}), bf16[1024,4096]{0,1:T(8,128)(2,1)}) %all-gather.3.cloned.1.call-update) | async-done | bytes 8388624 | tf_op jit(solution)/shard_map/all_gather | solution.py:57
  145.7 8.3 %fusion = f32[1024,512]{0,1:T(8,128)S(1)} fusion(bf16[1024,4096]{0,1:T(8,128)(2,1)} %all-gather.3.cloned.1.call-done, bf16[4096,256]{1,0:T(8,128)(2,1)} %get-tuple-element.9, bf16[4096,256]{1,0:T(8,128)(2,1)} %get-tuple-element.8), kind=kOutput, calls=%fused_computation | convolution fusion | flops 4303355904 | bytes 14680064 | tf_op jit(solution)/shard_map/dot_general | solution.py:56
  154.0 0.0 copy-start
  154.0 5.8 %all_to_all.5 = f32[2,1024,256]{1,2,0:T(8,128)S(1)} all-to-all(f32[2,1024,256]{1,2,0:T(8,128)S(1)} %bitcast.34), channel_id=1, replica_groups=mesh['row'=8,'col_0'=4,'col_1'=4,'layer'=2] {'layer'}, dimensions={0} | all-to-all | bytes 4194304 | tf_op jit(solution)/shard_map/all_to_all | solution.py:28
  159.8 1.2 reduce_sum.18
  161.0 0.0 copy-done
  161.0 2.3 %select_reduce_fusion = (f32[]{:T(128)}, f32[1024,256]{0,1:T(8,128)S(1)}) fusion(s32[1024]{0:T(1024)S(1)} %iota_add_fusion, s32[256]{0:T(256)S(1)} %iota_add_fusion.1, f32[1024,2]{0,1:T(2,128)S(1)} %bitcast.35, f32[1024,256]{0,1:T(8,128)} %reduce_sum.18, bf16[1024,256]{0,1:T(8,128)(2,1)S(1)} %copy-done, pred[1024]{0:T(1024)(128)(4,1)S(1)} %broadcast_bitcast_fusion.2), kind=kLoop, calls=%fused_computation.8 | loop fusion | flops 2097151 | bytes 2635780 | tf_op jit(solution)/shard_map/reduce_sum | solution.py:72
  163.3 14.6 %psum.28 = f32[]{:T(128)} all-reduce(f32[]{:T(128)} %get-tuple-element.6), channel_id=1, replica_groups=mesh['row'=8,'col_0'=4,'col_1'=4,'layer'=2] {'row'}, use_global_device_ids=true, to_apply=%region_2.3 | all-reduce | flops 1 | bytes 8 | tf_op jit(solution)/shard_map/psum | solution.py:33
  178.0 9.0 %psum.29 = f32[]{:T(128)} all-reduce(f32[]{:T(128)} %psum.28), channel_id=1, replica_groups=mesh['row'=8,'col_0'=4,'col_1'=4,'layer'=2] {'col_0'}, use_global_device_ids=true, to_apply=%region_3.4 | all-reduce | flops 1 | bytes 8 | tf_op jit(solution)/shard_map/psum | solution.py:33
  187.0 7.2 %psum.30 = f32[]{:T(128)} all-reduce(f32[]{:T(128)} %psum.29), channel_id=1, replica_groups=mesh['row'=8,'col_0'=4,'col_1'=4,'layer'=2] {'col_1'}, use_global_device_ids=true, to_apply=%region_4.5 | all-reduce | flops 1 | bytes 8 | tf_op jit(solution)/shard_map/psum | solution.py:33
  194.2 1.3 copy.13
  195.5 10.6 %psum.31 = f32[]{:T(128)} all-reduce(f32[]{:T(128)} %psum.30), channel_id=1, replica_groups=mesh['row'=8,'col_0'=4,'col_1'=4,'layer'=2] {'layer'}, use_global_device_ids=true, to_apply=%region_5.6 | all-reduce | flops 1 | bytes 8 | tf_op jit(solution)/shard_map/psum | solution.py:33
  (8 shorter events, 0.0 us)
Async XLA Ops:
  7.2 61.7 %all-gather.5.cloned.1.call-start = ((), (), s32[]{:S(2)}) async-start(), calls=%async_computation.2 | async-start | bytes 4718592 | tf_op jit(solution)/shard_map/all_gather | solution.py:44
  10.1 135.6 %all-gather.3.cloned.1.call-start = ((), (), s32[]{:S(2)}) async-start(), calls=%async_computation.1 | async-start | bytes 8912896 | tf_op jit(solution)/shard_map/all_gather | solution.py:57
  90.1 11.2 %copy-start.1 = (s32[8,2]{0,1:T(2,128)S(1)}, s32[8,2]{0,1:T(2,128)}, u32[]{:S(2)}) copy-start(s32[8,2]{0,1:T(2,128)} %param.6) | copy-start | bytes 196
  90.1 11.3 %copy-start.2 = (s32[8]{0:T(128)S(1)}, s32[8]{0:T(128)}, u32[]{:S(2)}) copy-start(s32[8]{0:T(128)} %param.7) | copy-start | bytes 100
  100.6 9.8 %collective-permute-start = (bf16[16,256,256]{2,1,0:T(8,128)(2,1)}, bf16[16,256,256]{2,1,0:T(8,128)(2,1)}, u32[]{:S(2)}, u32[]{:S(2)}) collective-permute-start(bf16[16,256,256]{2,1,0:T(8,128)(2,1)} %bitcast.3), channel_id=1, source_target_pairs={{0,1},{1,0},{2,3},{3,2},{4,5},{5,4},{6,7},{7,6},{8,9},{9,8},{10,11... | collective-permute-start | bytes 6291464 | tf_op jit(solution)/shard_map/ppermute | solution.py:17
  154.0 7.1 %copy-start = (bf16[1024,256]{0,1:T(8,128)(2,1)S(1)}, bf16[1024,256]{0,1:T(8,128)(2,1)}, u32[]{:S(2)}) copy-start(bf16[1024,256]{0,1:T(8,128)(2,1)} %bitcast_multiply_fusion) | copy-start | bytes 1572868
Sparse Core Ops, SparseCore 0:
  10.2 58.6 all-gather.4
  71.3 74.3 all-gather.2
where the time goes:
time: 214 us; the launch traced here: 213 us
  waiting for transfers between devices  90.1 us (42%)
  blocking collectives  47.2 us (22%)
  local copies, waits for them, and re-layouts  43.5 us (20%)
  between operations  14.1 us (7%)
  other arithmetic  8.9 us (4%)
  matrix products  8.26 us (4%)
    all_gather x1, waiting for transfers between devices, on_device(): col_panel = lax.all_gather(masked, 'row', axis=0, tiled=True)  58 us
    psum x4, blocking collectives, over_axes(): return functools.reduce(lax.psum, axes, value)  41.4 us
    all_gather x1, waiting for transfers between devices, on_device(): lax.all_gather(masked, COL, axis=1, tiled=True)  31.4 us
    unnamed x14, local copies, waits for them, and re-layouts  22.2 us
    dynamic_slice x1, local copies, waits for them, and re-layouts, on_device(): own_rows = lax.dynamic_index_in_dim(grouped, layer_index, 1, keepdims=False)  13.4 us
    dot_general x1, matrix products, on_device(): jnp.dot(lax.all_gather(masked, COL, axis=1, tiled=True), inner_panel, pre...  8.26 us
    reshape x1, local copies, waits for them, and re-layouts, on_device(): grouped = col_panel.reshape(col_groups, 2, col_width, col_width)  7.82 us
    all_to_all x1, blocking collectives, sum_at_owner(): lax.all_to_all(split_up(value, dim, devices), axis, 0, 0, tiled=True)  5.85 us
  transfers between devices with their start and end apart: 3, of which 2 were waited for; matrix products, arithmetic and copies ran while one was open for 21% of the time, Pallas kernels for 0%

commit v1 on v0

--- a/solution.py
+++ b/solution.py
@@ -4,11 +4,18 @@
 from jax import lax
 from jax.sharding import Mesh
 from jax.sharding import PartitionSpec as P
+from jax.lax import axis_index, axis_size, ppermute
 
 BLK = 128
 COL = ("col_0", "col_1")
 ROW_COL_LAYER = ("row", "col_0", "col_1", "layer")
 COL_LAYER = ("col_0", "col_1", "layer")
+
+
+def read_kinds_by_axis(inner_x, join_dim):
+    inter = list(inner_x.shape[1:])
+    inter[join_dim] *= inner_x.shape[0]
+    return jnp.moveaxis(inner_x, 0, join_dim).reshape(inter)
 
 
 def partner(value, axis, stride):
@@ -41,7 +48,23 @@
     row_count = density.shape[0]
     col_width = density.shape[1]
     masked = density * expand_mask(block_mask).astype(jnp.bfloat16)
-    col_panel = lax.all_gather(masked, "row", axis=0, tiled=True)
+
+    def _begin_points(vec, group_axis, along_dim):
+        devs = axis_size(group_axis)
+        made = [(hop_no, (hop_no + 1) % devs) for hop_no in range(devs)]
+        store = [(to_i, h) for h, to_i in made]
+        v_now, item_now = ([], [])
+        for pp in range(devs - 1):
+            if pp % 2 == 0:
+                v_now.append(ppermute(v_now[-1] if v_now else vec, group_axis, made))
+            else:
+                item_now.append(ppermute(item_now[-1] if item_now else vec, group_axis, store))
+        val2 = jnp.stack([*v_now[::-1], vec, *item_now], 0)
+        ready = axis_index(group_axis) - len(v_now)
+        val2 = val2[(jnp.arange(devs) - ready) % devs]
+        return read_kinds_by_axis(val2, along_dim)
+
+    col_panel = _begin_points(masked, "row", 0)
     layer_index = lax.axis_index("layer")
     col_groups = lax.axis_size(COL)
     grouped = col_panel.reshape(col_groups, 2, col_width, col_width)

time: 214 us -> 168 us (0.79)
  waiting for transfers between devices: 90.1 us -> 49.5 us
  local copies, waits for them, and re-layouts: 43.5 us -> 26.2 us
  starting transfers between devices: 0.75 us -> 14.5 us
    all_gather x1 -> x0, waiting for transfers between devices: 58 us -> none  [on_device(): col_panel = lax.all_gather(masked, 'row', axis=0, tiled=True)]
    ppermute x0 -> x7, waiting for transfers between devices: none -> 45.5 us  [the longest x4 45.5 us: _begin_points(): v_now.append(ppermute(v_now[-1] if v_now else vec, group_axis, made))]
    all_gather x1, waiting for transfers between devices: 31.4 us -> 0.01 us  [on_device(): lax.all_gather(masked, COL, axis=1, tiled=True)]
    unnamed x14 -> x19, local copies, waits for them, and re-layouts: 22.2 us -> 9.76 us
    gather x0 -> x2, local copies, waits for them, and re-layouts: none -> 11.6 us  [_begin_points(): val2 = val2[(jnp.arange(devs) - ready) % devs]]
    ppermute x0 -> x7, starting transfers between devices: none -> 10.6 us  [the longest x3 8.1 us: _begin_points(): ppermute(item_now[-1] if item_now else vec, group_axis, store)]
    dynamic_slice x1, local copies, waits for them, and re-layouts: 13.4 us -> 3.97 us  [on_device(): own_rows = lax.dynamic_index_in_dim(grouped, layer_index, 1, keepdims=False)]
    reshape x1 -> x0, local copies, waits for them, and re-layouts: 7.82 us -> none  [on_device(): grouped = col_panel.reshape(col_groups, 2, col_width, col_width)]
  transfers between devices with their start and end apart: 3 -> 9, of which waited for: 2 -> 5; matrix products, arithmetic and copies ran while one was open for 21% -> 16% of each run, Pallas kernels for 0% -> 0%
where the time goes in v1:
time: 168 us; the launch traced here: 167 us
  waiting for transfers between devices  49.5 us (29%)
  blocking collectives  45.6 us (27%)
  local copies, waits for them, and re-layouts  26.2 us (16%)
  starting transfers between devices  14.5 us (9%)
  between operations  14.1 us (8%)
  other arithmetic  9.02 us (5%)
  matrix products  8.26 us (5%)
    ppermute x4, waiting for transfers between devices, _begin_points(): v_now.append(ppermute(v_now[-1] if v_now else vec, group_axis, made))  45.5 us
    psum x4, blocking collectives, over_axes(): return functools.reduce(lax.psum, axes, value)  40.2 us
    gather x2, local copies, waits for them, and re-layouts, _begin_points(): val2 = val2[(jnp.arange(devs) - ready) % devs]  11.6 us
    unnamed x19, local copies, waits for them, and re-layouts  9.76 us
    dot_general x1, matrix products, on_device(): jnp.dot(lax.all_gather(masked, COL, axis=1, tiled=True), inner_panel, pre...  8.26 us
    ppermute x3, starting transfers between devices, _begin_points(): ppermute(item_now[-1] if item_now else vec, group_axis, store)  8.1 us
    all_to_all x1, blocking collectives, sum_at_owner(): lax.all_to_all(split_up(value, dim, devices), axis, 0, 0, tiled=True)  5.42 us
    dynamic_slice x1, local copies, waits for them, and re-layouts, on_device(): own_rows = lax.dynamic_index_in_dim(grouped, layer_index, 1, keepdims=False)  3.97 us
  transfers between devices with their start and end apart: 9, of which 5 were waited for; matrix products, arithmetic and copies ran while one was open for 16% of the time, Pallas kernels for 0%

profile of v1, /device:TPU:1, one launch (start us, length us, event | category | flops | bytes accessed | tf_op | source)
XLA Modules:
  0.0 167.2 jit_solution(3964422031386870217)
XLA Ops:
  7.2 1.2 copy.10
  9.2 0.8 bitcast_multiply_fusion
  10.1 2.5 %collective-permute-start = (bf16[1024,256]{0,1:T(8,128)(2,1)}, bf16[1024,256]{0,1:T(8,128)(2,1)S(1)}, u32[]{:S(2)}, u32[]{:S(2)}) collective-permute-start(bf16[1024,256]{0,1:T(8,128)(2,1)} %bitcast_multiply_fusion), channel_id=1, source_target_pairs={{0,32},{32,64},{64,96},{96,128},{128,160},{160,192},{192,224},{224... | collective-permute-start | bytes 1572872 | tf_op jit(solution)/shard_map/ppermute | solution.py:59
  12.6 15.8 %collective-permute-done = bf16[1024,256]{0,1:T(8,128)(2,1)S(1)} collective-permute-done((bf16[1024,256]{0,1:T(8,128)(2,1)}, bf16[1024,256]{0,1:T(8,128)(2,1)S(1)}, u32[]{:S(2)}, u32[]{:S(2)}) %collective-permute-start) | collective-permute-done | bytes 524320 | tf_op jit(solution)/shard_map/ppermute | solution.py:59
  28.4 2.7 %collective-permute-start.4 = (bf16[1024,256]{0,1:T(8,128)(2,1)}, bf16[1024,256]{0,1:T(8,128)(2,1)S(1)}, u32[]{:S(2)}, u32[]{:S(2)}) collective-permute-start(bf16[1024,256]{0,1:T(8,128)(2,1)} %bitcast_multiply_fusion), channel_id=1, source_target_pairs={{32,0},{64,32},{96,64},{128,96},{160,128},{192,160},{224,192},{0,2... | collective-permute-start | bytes 1572872 | tf_op jit(solution)/shard_map/ppermute | solution.py:61
  31.1 10.8 %collective-permute-done.1 = bf16[1024,256]{0,1:T(8,128)(2,1)S(1)} collective-permute-done((bf16[1024,256]{0,1:T(8,128)(2,1)S(1)}, bf16[1024,256]{0,1:T(8,128)(2,1)S(1)}, u32[]{:S(2)}, u32[]{:S(2)}) %collective-permute-start.1) | collective-permute-done | bytes 524320 | tf_op jit(solution)/shard_map/ppermute | solution.py:59
  41.9 2.7 %collective-permute-start.5 = (bf16[1024,256]{0,1:T(8,128)(2,1)S(1)}, bf16[1024,256]{0,1:T(8,128)(2,1)S(1)}, u32[]{:S(2)}, u32[]{:S(2)}) collective-permute-start(bf16[1024,256]{0,1:T(8,128)(2,1)S(1)} %collective-permute-done.4), channel_id=1, source_target_pairs={{32,0},{64,32},{96,64},{128,96},{160,128},{192,160},{224,192},{0,2... | collective-permute-start | bytes 1572872 | tf_op jit(solution)/shard_map/ppermute | solution.py:61
  44.6 9.9 %collective-permute-done.2 = bf16[1024,256]{0,1:T(8,128)(2,1)S(1)} collective-permute-done((bf16[1024,256]{0,1:T(8,128)(2,1)S(1)}, bf16[1024,256]{0,1:T(8,128)(2,1)S(1)}, u32[]{:S(2)}, u32[]{:S(2)}) %collective-permute-start.2) | collective-permute-done | bytes 524320 | tf_op jit(solution)/shard_map/ppermute | solution.py:59
  54.6 2.7 %collective-permute-start.6 = (bf16[1024,256]{0,1:T(8,128)(2,1)S(1)}, bf16[1024,256]{0,1:T(8,128)(2,1)S(1)}, u32[]{:S(2)}, u32[]{:S(2)}) collective-permute-start(bf16[1024,256]{0,1:T(8,128)(2,1)S(1)} %collective-permute-done.5), channel_id=1, source_target_pairs={{32,0},{64,32},{96,64},{128,96},{160,128},{192,160},{224,192},{0,2... | collective-permute-start | bytes 1572872 | tf_op jit(solution)/shard_map/ppermute | solution.py:61
  57.3 9.0 %collective-permute-done.3 = bf16[1024,256]{0,1:T(8,128)(2,1)} collective-permute-done((bf16[1024,256]{0,1:T(8,128)(2,1)S(1)}, bf16[1024,256]{0,1:T(8,128)(2,1)}, u32[]{:S(2)}, u32[]{:S(2)}) %collective-permute-start.3) | collective-permute-done | bytes 524320 | tf_op jit(solution)/shard_map/ppermute | solution.py:59
  66.3 1.9 %bitcast_dynamic-update-slice_fusion.7 = bf16[8,1024,256]{1,2,0:T(8,128)(2,1)} fusion(bf16[1024,256]{0,1:T(8,128)(2,1)} %collective-permute-done.3), kind=kLoop, calls=%fused_computation.18 | loop fusion | bytes 1048576
  68.2 0.9 bitcast_dynamic-update-slice_fusion.6
  69.1 0.8 bitcast_dynamic-update-slice_fusion.5
  70.8 0.9 bitcast_dynamic-update-slice_fusion.3
  71.6 0.8 bitcast_dynamic-update-slice_fusion.2
  72.5 0.8 bitcast_dynamic-update-slice_fusion.1
  73.3 0.8 bitcast_dynamic-update-slice_fusion
  74.2 5.1 %gather_fusion = bf16[8,1024,256]{1,2,0:T(8,128)(2,1)} fusion(bf16[8,1024,256]{1,2,0:T(8,128)(2,1)} %bitcast_dynamic-update-slice_fusion, s32[1024]{0:T(1024)S(1)} %pad_clamp_fusion), kind=kCustom, calls=%fused_computation | custom fusion | bytes 8388640 | tf_op jit(solution)/shard_map/gather | solution.py:64
  79.2 6.5 %copy.11 = bf16[8,1024,256]{2,1,0:T(8,128)(2,1)} copy(bf16[8,1024,256]{1,2,0:T(8,128)(2,1)} %gather_fusion) | data formatting | bytes 8388608 | tf_op jit(solution)/shard_map/gather | solution.py:64
  85.7 4.0 %constant_dynamic-slice_fusion = (bf16[16,1,256,256]{3,2,1,0:T(8,128)(2,1)S(1)}, bf16[16,256,256]{2,1,0:T(8,128)(2,1)}) fusion(bf16[16,2,256,256]{3,2,1,0:T(8,128)(2,1)} %bitcast.52, s32[]{:T(128)S(6)} %select_n.54, s32[]{:T(128)S(6)} %select_n.55), kind=kLoop, calls=%fused_computation.34 | loop fusion | bytes 8388616 | tf_op jit(solution)/shard_map/jit(dynamic_index_in_dim)/dynamic_slice | solution.py:71
  89.7 3.8 %collective-permute-start.7 = (bf16[16,256,256]{2,1,0:T(8,128)(2,1)}, bf16[16,256,256]{2,1,0:T(8,128)(2,1)}, u32[]{:S(2)}, u32[]{:S(2)}) collective-permute-start(bf16[16,256,256]{2,1,0:T(8,128)(2,1)} %get-tuple-element.11), channel_id=1, source_target_pairs={{0,1},{1,0},{2,3},{3,2},{4,5},{5,4},{6,7},{7,6},{8,9},{9,8},{10,11... | collective-permute-start | bytes 6291464 | tf_op jit(solution)/shard_map/ppermute | solution.py:24
  93.8 3.9 %collective-permute-done.7 = bf16[16,256,256]{2,1,0:T(8,128)(2,1)} collective-permute-done((bf16[16,256,256]{2,1,0:T(8,128)(2,1)}, bf16[16,256,256]{2,1,0:T(8,128)(2,1)}, u32[]{:S(2)}, u32[]{:S(2)}) %collective-permute-start.7) | collective-permute-done | bytes 2097184 | tf_op jit(solution)/shard_map/ppermute | solution.py:24
  97.7 3.9 %bitcast_select_fusion.1 = (bf16[4096,256]{1,0:T(8,128)(2,1)}, bf16[4096,256]{1,0:T(8,128)(2,1)}) fusion(bf16[16,256,256]{2,1,0:T(8,128)(2,1)} %collective-permute-done.7, bf16[16,1,256,256]{3,2,1,0:T(8,128)(2,1)S(1)} %get-tuple-element.10, pred[]{:T(512)S(6)} %eq.37), kind=kLoop, calls=%fused_computation.6 | loop fusion | flops 2097152 | bytes 8388609 | tf_op jit(solution)/shard_map/jit(_where)/select_n | solution.py:76
  101.6 8.3 %fusion = f32[1024,512]{0,1:T(8,128)S(1)} fusion(bf16[1024,4096]{0,1:T(8,128)(2,1)} %all-gather.2.cloned.1.call-done, bf16[4096,256]{1,0:T(8,128)(2,1)} %get-tuple-element.9, bf16[4096,256]{1,0:T(8,128)(2,1)} %get-tuple-element.8), kind=kOutput, calls=%fused_computation.1 | convolution fusion | flops 4303355904 | bytes 14680064 | tf_op jit(solution)/shard_map/dot_general | solution.py:79
  109.9 5.4 %all_to_all.5 = f32[2,1024,256]{1,2,0:T(8,128)S(1)} all-to-all(f32[2,1024,256]{1,2,0:T(8,128)S(1)} %bitcast.53), channel_id=1, replica_groups=mesh['row'=8,'col_0'=4,'col_1'=4,'layer'=2] {'layer'}, dimensions={0} | all-to-all | bytes 4194304 | tf_op jit(solution)/shard_map/all_to_all | solution.py:35
  115.3 1.2 reduce_sum.18
  116.5 2.3 %select_reduce_fusion = (f32[]{:T(128)}, f32[1024,256]{0,1:T(8,128)S(1)}) fusion(s32[1024]{0:T(1024)S(1)} %iota_add_fusion, s32[256]{0:T(256)S(1)} %iota_add_fusion.1, f32[1024,2]{0,1:T(2,128)S(1)} %bitcast.54, f32[1024,256]{0,1:T(8,128)} %reduce_sum.18, bf16[1024,256]{0,1:T(8,128)(2,1)S(1)} %copy-done, pred[1024]{0:T(1024)(128)(4,1)S(1)} %broadcast_bitcast_fusion.2), kind=kLoop, calls=%fused_computation.10 | loop fusion | flops 2097151 | bytes 2635780 | tf_op jit(solution)/shard_map/reduce_sum | solution.py:95
  118.8 11.4 %psum.28 = f32[]{:T(128)} all-reduce(f32[]{:T(128)} %get-tuple-element.6), channel_id=1, replica_groups=mesh['row'=8,'col_0'=4,'col_1'=4,'layer'=2] {'row'}, use_global_device_ids=true, to_apply=%region_2.3 | all-reduce | flops 1 | bytes 8 | tf_op jit(solution)/shard_map/psum | solution.py:40
  130.2 9.3 %psum.29 = f32[]{:T(128)} all-reduce(f32[]{:T(128)} %psum.28), channel_id=1, replica_groups=mesh['row'=8,'col_0'=4,'col_1'=4,'layer'=2] {'col_0'}, use_global_device_ids=true, to_apply=%region_3.4 | all-reduce | flops 1 | bytes 8 | tf_op jit(solution)/shard_map/psum | solution.py:40
  139.6 8.9 %psum.30 = f32[]{:T(128)} all-reduce(f32[]{:T(128)} %psum.29), channel_id=1, replica_groups=mesh['row'=8,'col_0'=4,'col_1'=4,'layer'=2] {'col_1'}, use_global_device_ids=true, to_apply=%region_4.5 | all-reduce | flops 1 | bytes 8 | tf_op jit(solution)/shard_map/psum | solution.py:40
  148.5 1.3 copy.12
  149.8 10.5 %psum.31 = f32[]{:T(128)} all-reduce(f32[]{:T(128)} %psum.30), channel_id=1, replica_groups=mesh['row'=8,'col_0'=4,'col_1'=4,'layer'=2] {'layer'}, use_global_device_ids=true, to_apply=%region_5.6 | all-reduce | flops 1 | bytes 8 | tf_op jit(solution)/shard_map/psum | solution.py:40
  (28 shorter events, 1.9 us)
Async XLA Ops:
  7.2 94.5 %all-gather.2.cloned.1.call-start = ((), (), s32[]{:S(2)}) async-start(), calls=%async_computation.1 | async-start | bytes 8912896 | tf_op jit(solution)/shard_map/all_gather | solution.py:80
  10.1 60.7 %copy-start = (bf16[1024,256]{0,1:T(8,128)(2,1)S(1)}, bf16[1024,256]{0,1:T(8,128)(2,1)}, u32[]{:S(2)}) copy-start(bf16[1024,256]{0,1:T(8,128)(2,1)} %bitcast_multiply_fusion) | copy-start | bytes 1572868
  10.1 18.3 %collective-permute-start = (bf16[1024,256]{0,1:T(8,128)(2,1)}, bf16[1024,256]{0,1:T(8,128)(2,1)S(1)}, u32[]{:S(2)}, u32[]{:S(2)}) collective-permute-start(bf16[1024,256]{0,1:T(8,128)(2,1)} %bitcast_multiply_fusion), channel_id=1, source_target_pairs={{0,32},{32,64},{64,96},{96,128},{128,160},{160,192},{192,224},{224... | collective-permute-start | bytes 1572872 | tf_op jit(solution)/shard_map/ppermute | solution.py:59
  28.4 13.5 %collective-permute-start.1 = (bf16[1024,256]{0,1:T(8,128)(2,1)S(1)}, bf16[1024,256]{0,1:T(8,128)(2,1)S(1)}, u32[]{:S(2)}, u32[]{:S(2)}) collective-permute-start(bf16[1024,256]{0,1:T(8,128)(2,1)S(1)} %collective-permute-done), channel_id=1, source_target_pairs={{0,32},{32,64},{64,96},{96,128},{128,160},{160,192},{192,224},{224... | collective-permute-start | bytes 1572872 | tf_op jit(solution)/shard_map/ppermute | solution.py:59
  28.4 13.5 %collective-permute-start.4 = (bf16[1024,256]{0,1:T(8,128)(2,1)}, bf16[1024,256]{0,1:T(8,128)(2,1)S(1)}, u32[]{:S(2)}, u32[]{:S(2)}) collective-permute-start(bf16[1024,256]{0,1:T(8,128)(2,1)} %bitcast_multiply_fusion), channel_id=1, source_target_pairs={{32,0},{64,32},{96,64},{128,96},{160,128},{192,160},{224,192},{0,2... | collective-permute-start | bytes 1572872 | tf_op jit(solution)/shard_map/ppermute | solution.py:61
  41.9 12.6 %collective-permute-start.2 = (bf16[1024,256]{0,1:T(8,128)(2,1)S(1)}, bf16[1024,256]{0,1:T(8,128)(2,1)S(1)}, u32[]{:S(2)}, u32[]{:S(2)}) collective-permute-start(bf16[1024,256]{0,1:T(8,128)(2,1)S(1)} %collective-permute-done.1), channel_id=1, source_target_pairs={{0,32},{32,64},{64,96},{96,128},{128,160},{160,192},{192,224},{224... | collective-permute-start | bytes 1572872 | tf_op jit(solution)/shard_map/ppermute | solution.py:59
  41.9 12.6 %collective-permute-start.5 = (bf16[1024,256]{0,1:T(8,128)(2,1)S(1)}, bf16[1024,256]{0,1:T(8,128)(2,1)S(1)}, u32[]{:S(2)}, u32[]{:S(2)}) collective-permute-start(bf16[1024,256]{0,1:T(8,128)(2,1)S(1)} %collective-permute-done.4), channel_id=1, source_target_pairs={{32,0},{64,32},{96,64},{128,96},{160,128},{192,160},{224,192},{0,2... | collective-permute-start | bytes 1572872 | tf_op jit(solution)/shard_map/ppermute | solution.py:61
  54.5 11.8 %collective-permute-start.3 = (bf16[1024,256]{0,1:T(8,128)(2,1)S(1)}, bf16[1024,256]{0,1:T(8,128)(2,1)}, u32[]{:S(2)}, u32[]{:S(2)}) collective-permute-start(bf16[1024,256]{0,1:T(8,128)(2,1)S(1)} %collective-permute-done.2), channel_id=1, source_target_pairs={{0,32},{32,64},{64,96},{96,128},{128,160},{160,192},{192,224},{224... | collective-permute-start | bytes 1572872 | tf_op jit(solution)/shard_map/ppermute | solution.py:59
  54.6 18.8 %collective-permute-start.6 = (bf16[1024,256]{0,1:T(8,128)(2,1)S(1)}, bf16[1024,256]{0,1:T(8,128)(2,1)S(1)}, u32[]{:S(2)}, u32[]{:S(2)}) collective-permute-start(bf16[1024,256]{0,1:T(8,128)(2,1)S(1)} %collective-permute-done.5), channel_id=1, source_target_pairs={{32,0},{64,32},{96,64},{128,96},{160,128},{192,160},{224,192},{0,2... | collective-permute-start | bytes 1572872 | tf_op jit(solution)/shard_map/ppermute | solution.py:61
  85.7 7.8 %copy-start.1 = (s32[8,2]{0,1:T(2,128)S(1)}, s32[8,2]{0,1:T(2,128)}, u32[]{:S(2)}) copy-start(s32[8,2]{0,1:T(2,128)} %param.6) | copy-start | bytes 196
  85.7 7.9 %copy-start.2 = (s32[8]{0:T(128)S(1)}, s32[8]{0:T(128)}, u32[]{:S(2)}) copy-start(s32[8]{0:T(128)} %param.7) | copy-start | bytes 100
  89.7 8.0 %collective-permute-start.7 = (bf16[16,256,256]{2,1,0:T(8,128)(2,1)}, bf16[16,256,256]{2,1,0:T(8,128)(2,1)}, u32[]{:S(2)}, u32[]{:S(2)}) collective-permute-start(bf16[16,256,256]{2,1,0:T(8,128)(2,1)} %get-tuple-element.11), channel_id=1, source_target_pairs={{0,1},{1,0},{2,3},{3,2},{4,5},{5,4},{6,7},{7,6},{8,9},{9,8},{10,11... | collective-permute-start | bytes 6291464 | tf_op jit(solution)/shard_map/ppermute | solution.py:24
Sparse Core Ops, SparseCore 0:
  11.0 79.5 all-gather.1
